TPU v7x, 32 devices: a whole 2x2x4 slice. The times are simulated.
32 devices in a mesh: dp: 4 (over z), row: 2 (over core), col: 4 (over y, x).
Axes of the slice: x: 2, y: 2, z: 4, core: 2. Of those that a mesh axis runs over, the one named last changes fastest.
Arguments:
- features: bfloat16 [2048, 4096], P(('dp', 'row')), may hold values from -6 to 6
- w_in: bfloat16 [4096, 4096], P('row', 'col'), may hold values from -0.09375 to 0.09375
- w_out: bfloat16 [4096, 1024], P('col'), may hold values from -0.09375 to 0.09375
- captions: bfloat16 [2048, 1024], P(('dp', 'row', 'col')), may hold values from -6 to 6
- positive: int32 [2048], P(('dp', 'row')), may hold values from 0 to 2047, each once
Outputs:
- fig_terms: float32 [2048], P(('dp', 'row'))
- cap_terms: float32 [2048], P(('dp', 'row', 'col'))
- grad_w_in: float32 [4096, 4096], P(('dp', 'row'), 'col')
- grad_w_out: float32 [4096, 1024], P('col', ('dp', 'row'))
Inputs may be any that keep to these rules, and one draw needn't show every extreme that they name: positive is a permutation: every caption is the match of exactly one figure.
All inputs are finite; a program needn't handle non-finite values.
Results may differ from a plain program's by a relative error of at most 0.0053.
Values may be sent and summed in bfloat16 or wider, within the bound.
A program may use at most 128 MiB of HBM per device.

v0:
```python
import jax
import jax.numpy as jnp
from jax import lax
from jax.sharding import PartitionSpec as P

SCALE = 50.0
EPS = 1e-06


def gelu_back(pre, grad):
    return jax.vjp(jax.nn.gelu, pre)[1](grad)[0]


def on_device(features, w_in, w_out, captions, positive):
    group = ("dp", "row")
    every = ("dp", "row", "col")
    f32 = jnp.float32
    slices = lax.all_to_all(features, group, 1, 0, tiled=True)
    cap32 = captions.astype(f32)
    chat_local = (cap32 * lax.rsqrt(jnp.sum(cap32 * cap32, axis=1, keepdims=True) + EPS)).astype(
        jnp.bfloat16
    )
    chat = lax.all_gather(chat_local, every, axis=0, tiled=True)
    pre = jnp.dot(
        features, lax.all_gather(w_in, "row", axis=0, tiled=True), preferred_element_type=f32
    )
    hidden = jax.nn.gelu(pre).astype(jnp.bfloat16)
    part = jnp.dot(hidden, w_out, preferred_element_type=f32)
    emb = lax.psum_scatter(part, "col", scatter_dimension=0, tiled=True)
    mine = emb.shape[0]
    inv = lax.rsqrt(jnp.sum(emb * emb, axis=1, keepdims=True) + EPS)
    fhat = emb * inv
    fhat_b = fhat.astype(jnp.bfloat16)
    logits = SCALE * lax.dot_general(
        fhat_b, chat, (((1,), (1,)), ((), ())), preferred_element_type=f32
    )
    col = lax.axis_index("col")
    places = lax.dynamic_slice_in_dim(positive, col * mine, mine, 0)
    colids = jnp.arange(chat.shape[0], dtype=jnp.int32)
    mask = (places[:, None] == colids[None, :]).astype(f32)
    expo = jnp.exp(logits)
    picked = mask * logits
    rowsum, rowpos = (jnp.sum(expo, axis=1), jnp.sum(picked, axis=1))
    colsum, colpos = lax.psum((jnp.sum(expo, axis=0), jnp.sum(picked, axis=0)), every)
    fig_terms = lax.all_gather(jnp.log(rowsum) - rowpos, "col", axis=0, tiled=True)
    capdev = captions.shape[0]
    place = (lax.axis_index("dp") * lax.axis_size("row") + lax.axis_index("row")) * lax.axis_size(
        "col"
    ) + col
    cap_terms = lax.dynamic_slice_in_dim(jnp.log(colsum) - colpos, place * capdev, capdev, 0)
    dlog = (expo / rowsum[:, None] + expo / colsum[None, :] - 2.0 * mask).astype(jnp.bfloat16)
    dfhat = SCALE * jnp.dot(dlog, chat, preferred_element_type=f32)
    demb = ((dfhat - fhat * jnp.sum(fhat * dfhat, axis=1, keepdims=True)) * inv).astype(
        jnp.bfloat16
    )
    demb = lax.all_gather(demb, "col", axis=0, tiled=True)
    dh = lax.dot_general(demb, w_out, (((1,), (1,)), ((), ())), preferred_element_type=f32)
    dpre = gelu_back(pre, dh).astype(jnp.bfloat16)
    dpre_all = lax.all_gather(dpre, group, axis=0, tiled=True)
    head_term = lax.dot_general(hidden, demb, (((0,), (0,)), ((), ())), preferred_element_type=f32)
    grad_w_out = lax.psum_scatter(head_term, group, scatter_dimension=1, tiled=True)
    grad_w_in = lax.dot_general(
        slices, dpre_all, (((0,), (0,)), ((), ())), preferred_element_type=f32
    )
    return (fig_terms, cap_terms, grad_w_in, grad_w_out)


def solution(mesh):
    placed = (
        P(("dp", "row"), None),
        P("row", "col"),
        P("col", None),
        P(("dp", "row", "col"), None),
        P(("dp", "row")),
    )
    return jax.shard_map(
        on_device,
        mesh=mesh,
        in_specs=placed,
        out_specs=(
            P(("dp", "row")),
            P(("dp", "row", "col")),
            P(("dp", "row"), "col"),
            P("col", ("dp", "row")),
        ),
        check_vma=False,
    )
```

profile of v0, /device:TPU:0, one launch (start us, length us, event | category | flops | bytes accessed | tf_op | source)
XLA Modules:
  0.0 310.4 jit_solution(15779341503108276041)
XLA Ops:
  8.0 0.0 copy-start
  8.0 0.0 all-gather.4.cloned.1.call-start
  8.1 0.7 all-gather.4.cloned.1.call-update
  8.7 0.0 reduce-scatter.3.cloned.1.call-start
  8.8 24.2 %all-gather.4.cloned.1.call-done = bf16[4096,1024]{1,0:T(8,128)(2,1)} async-done(((bf16[2048,1024]{1,0:T(8,128)(2,1)}), bf16[4096,1024]{1,0:T(8,128)(2,1)}) %all-gather.4.cloned.1.call-update) | async-done | bytes 8388624 | tf_op jit(solution)/shard_map/all_gather | solution.py:25
  33.0 6.3 %fusion.22 = f32[256,1024]{1,0:T(8,128)S(1)} fusion(bf16[256,4096]{1,0:T(8,128)(2,1)} %param.5, bf16[4096,1024]{1,0:T(8,128)(2,1)} %all-gather.4.cloned.1.call-done), kind=kOutput, calls=%fused_computation.43 | convolution fusion | flops 2147483648 | bytes 11534336 | tf_op jit(solution)/shard_map/dot_general | solution.py:24
  39.3 0.0 copy-start.2
  39.3 1.1 copy-done.2
  40.4 0.0 copy-done
  40.4 0.0 copy-start.4
  40.4 0.0 copy-start.5
  40.4 1.8 fusion.21
  42.2 0.0 reduce-scatter.3.cloned.1.call-update
  42.2 0.0 all-gather.6.cloned.1.call-start
  42.3 0.0 copy-done.4
  42.3 0.1 fusion.10
  42.4 0.8 fusion.11
  43.2 0.0 all-gather.6.cloned.1.call-update
  43.2 0.0 all-gather.8.cloned.1.call-start
  43.3 0.0 copy-done.5
  43.3 0.1 dynamic_slice.6
  43.4 28.3 %reduce-scatter.3.cloned.1.call-done = f32[64,1024]{1,0:T(8,128)} async-done(((f32[256,1024]{1,0:T(8,128)}), f32[64,1024]{1,0:T(8,128)}) %reduce-scatter.3.cloned.1.call-update) | async-done | bytes 262160 | tf_op jit(solution)/shard_map/reduce_scatter | solution.py:29
  71.6 1.1 multiply_reduce_fusion.1
  72.7 0.0 copy-start.1
  72.7 36.8 %all-gather.6.cloned.1.call-done = bf16[2048,1024]{1,0:T(8,128)(2,1)} async-done(((bf16[64,1024]{1,0:T(8,128)(2,1)}), bf16[2048,1024]{1,0:T(8,128)(2,1)}) %all-gather.6.cloned.1.call-update) | async-done | bytes 4194320 | tf_op jit(solution)/shard_map/all_gather | solution.py:23
  109.5 3.9 %fusion.8 = (f32[2048]{0:T(1024)S(1)}, f32[64]{0:T(128)S(1)}, f32[2048]{0:T(1024)S(1)}, f32[64]{0:T(128)S(1)}, f32[64,2048]{1,0:T(8,128)S(1)}) fusion(s32[64]{0:T(128)S(1)} %dynamic_slice.6, bf16[2048,1024]{1,0:T(8,128)(2,1)} %all-gather.6.cloned.1.call-done, f32[64,1024]{1,0:T(8,128)} %reduce-scatter.3.cloned.1.call-done, f32[64]{0:T(128)S(1)} %add_rsqrt_fusion.1), kind=kOutput, calls=%fused_computation.16 | convolution fusion | flops 269479808 | bytes 4998144 | tf_op jit(solution)/shard_map/dot_general | solution.py:34
  113.4 39.3 %all-reduce.1 = (f32[2048]{0:T(1024)S(1)}, f32[2048]{0:T(1024)S(1)}) all-reduce(f32[2048]{0:T(1024)S(1)} %get-tuple-element.16, f32[2048]{0:T(1024)S(1)} %get-tuple-element.18), channel_id=1, replica_groups=mesh['dp'=4,'row'=2,'col'=4] {'dp','row','col'}, use_global_device_ids=true, to_apply=%region_8.0 | all-reduce | flops 4096 | bytes 32768 | tf_op jit(solution)/shard_map/psum | solution.py:44
  152.7 0.0 copy-done.1
  152.7 0.0 copy-start.3
  152.7 3.3 %multiply_reduce_fusion = (f32[64]{0:T(128)S(1)}, f32[64,1024]{1,0:T(8,128)S(1)}) fusion(f32[64,1024]{1,0:T(8,128)S(1)} %copy-done.1, f32[64]{0:T(128)S(1)} %add_rsqrt_fusion.1, bf16[2048,1024]{1,0:T(8,128)(2,1)} %all-gather.6.cloned.1.call-done, f32[64,2048]{1,0:T(8,128)S(1)} %get-tuple-element.22, f32[2048]{0:T(1024)S(1)} %get-tuple-element.21, ...), kind=kOutput, calls=%fused_computation.25 | convolution fusion | flops 269615040 | bytes 5252096 | tf_op jit(solution)/shard_map/dot_general | solution.py:52
  156.0 0.1 multiply_convert_fusion.1
  156.1 11.6 %all_gather.18 = bf16[256,1024]{1,0:T(8,128)(2,1)S(1)} all-gather(bf16[64,1024]{1,0:T(8,128)(2,1)S(1)} %multiply_convert_fusion.1), channel_id=1, replica_groups=mesh['dp'=4,'row'=2,'col'=4] {'col'}, dimensions={0}, use_global_device_ids=true | all-gather | bytes 655360 | tf_op jit(solution)/shard_map/all_gather | solution.py:56
  167.7 0.0 copy-done.3
  167.7 2.1 fusion.6
  169.8 0.0 all-gather.8.cloned.1.call-update
  169.8 0.0 reduce-scatter.5.cloned.1.call-start
  169.9 4.0 %fusion.20 = f32[1024,1024]{1,0:T(8,128)} fusion(bf16[256,1024]{1,0:T(8,128)(2,1)S(1)} %all_gather.18, f32[256,1024]{1,0:T(8,128)} %copy-done.2), kind=kOutput, calls=%fused_computation.41 | convolution fusion | flops 539230208 | bytes 5767168 | tf_op jit(solution)/shard_map/dot_general | solution.py:60
  173.9 0.0 reduce-scatter.5.cloned.1.call-update
  173.9 4.1 %copy.11 = bf16[256,4096]{0,1:T(8,128)(2,1)} copy(bf16[256,4096]{1,0:T(8,128)(2,1)} %param.5) | data formatting | bytes 4194304 | tf_op args[0]
  178.1 0.0 copy-start.6
  178.1 4.5 %all-to-all-start = ((bf16[256,8,512]{0,2,1:T(8,128)(2,1)}), bf16[256,8,512]{0,2,1:T(8,128)(2,1)}, u32[]{:S(2)}, u32[]{:S(2)}) async-start(bf16[256,8,512]{0,2,1:T(8,128)(2,1)} %bitcast.16), calls=%async_computation.1 | async-start | bytes 4194304 | tf_op jit(solution)/shard_map/all_to_all | solution.py:18
  182.6 0.0 copy-done.6
  182.6 0.6 dynamic-slice
  183.8 74.7 %all-to-all-done = bf16[256,8,512]{0,2,1:T(8,128)(2,1)} async-done(((bf16[256,8,512]{0,2,1:T(8,128)(2,1)}), bf16[256,8,512]{0,2,1:T(8,128)(2,1)}, u32[]{:S(2)}, u32[]{:S(2)}) %all-to-all-start) | async-done | bytes 2097184 | tf_op jit(solution)/shard_map/all_to_all | solution.py:18
  258.5 4.0 %copy.12 = bf16[8,256,512]{2,1,0:T(8,128)(2,1)} copy(bf16[8,256,512]{1,2,0:T(8,128)(2,1)} %bitcast.2) | data formatting | bytes 4194304 | tf_op jit(solution)/shard_map/all_to_all | solution.py:18
  262.5 0.1 subtract_dynamic-update-slice_fusion
  262.6 10.5 %all-reduce = f32[256]{0:T(256)} all-reduce(f32[256]{0:T(256)S(1)} %subtract_dynamic-update-slice_fusion), channel_id=1, replica_groups=mesh['dp'=4,'row'=2,'col'=4] {'col'}, use_global_device_ids=true, to_apply=%add | all-reduce | flops 256 | bytes 2048
  273.1 0.6 dynamic-slice_subtract_fusion
  273.7 0.0 all-gather.8.cloned.1.call-done
  273.7 6.7 %convolution_bitcast_fusion = f32[512,1024]{0,1:T(8,128)} fusion(bf16[2048,1024]{1,0:T(8,128)(2,1)} %all-gather.8.cloned.1.call-done, bf16[2048,512]{1,0:T(8,128)(2,1)} %bitcast.17), kind=kOutput, calls=%fused_computation.1 | convolution fusion | flops 2147483648 | bytes 8388608 | tf_op jit(solution)/shard_map/dot_general | solution.py:62
  280.4 2.9 copy.13
  283.3 19.6 %reduce-scatter.5.cloned.1.call-done = f32[1024,128]{1,0:T(8,128)} async-done(((f32[1024,1024]{1,0:T(8,128)}), f32[1024,128]{1,0:T(8,128)}) %reduce-scatter.5.cloned.1.call-update) | async-done | bytes 524304 | tf_op jit(solution)/shard_map/reduce_scatter | solution.py:61
  (3 shorter events, 0.0 us)
Async XLA Ops:
  8.0 32.4 %copy-start = (bf16[1024,1024]{1,0:T(8,128)(2,1)S(1)}, bf16[1024,1024]{1,0:T(8,128)(2,1)}, u32[]{:S(2)}) copy-start(bf16[1024,1024]{1,0:T(8,128)(2,1)} %param.7) | copy-start | bytes 6291460
  8.0 25.0 %all-gather.4.cloned.1.call-start = ((), (), s32[]{:S(2)}) async-start(), calls=%async_computation.3 | async-start | bytes 12582912 | tf_op jit(solution)/shard_map/all_gather | solution.py:25
  8.7 62.9 %reduce-scatter.3.cloned.1.call-start = ((), (), s32[]{:S(2)}) async-start(), calls=%async_computation.4 | async-start | bytes 1310720 | tf_op jit(solution)/shard_map/reduce_scatter | solution.py:29
  39.3 1.1 copy-start.2
  40.4 1.9 copy-start.4
  40.4 2.9 copy-start.5
  42.2 67.3 %all-gather.6.cloned.1.call-start = ((), (), s32[]{:S(2)}) async-start(), calls=%async_computation.5 | async-start | bytes 4325376 | tf_op jit(solution)/shard_map/all_gather | solution.py:23
  43.2 230.5 %all-gather.8.cloned.1.call-start = ((), (), s32[]{:S(2)}) async-start(), calls=%async_computation.6 | async-start | bytes 4718592 | tf_op jit(solution)/shard_map/all_gather | solution.py:59
  72.7 80.0 %copy-start.1 = (f32[64,1024]{1,0:T(8,128)S(1)}, f32[64,1024]{1,0:T(8,128)}, u32[]{:S(2)}) copy-start(f32[64,1024]{1,0:T(8,128)} %reduce-scatter.3.cloned.1.call-done) | copy-start | bytes 786436
  152.7 15.0 %copy-start.3 = (f32[256,1024]{1,0:T(8,128)S(1)}, f32[256,1024]{1,0:T(8,128)}, u32[]{:S(2)}) copy-start(f32[256,1024]{1,0:T(8,128)} %copy-done.2) | copy-start | bytes 3145732
  169.8 133.0 %reduce-scatter.5.cloned.1.call-start = ((), (), s32[]{:S(2)}) async-start(), calls=%async_computation.7 | async-start | bytes 4718592 | tf_op jit(solution)/shard_map/reduce_scatter | solution.py:61
  178.1 4.5 %copy-start.6 = (u32[32]{0:T(128)S(1)}, u32[32]{0:T(128)}, u32[]{:S(2)}) copy-start(u32[32]{0:T(128)} %constant.49) | copy-start | bytes 388
  178.1 80.4 %all-to-all-start = ((bf16[256,8,512]{0,2,1:T(8,128)(2,1)}), bf16[256,8,512]{0,2,1:T(8,128)(2,1)}, u32[]{:S(2)}, u32[]{:S(2)}) async-start(bf16[256,8,512]{0,2,1:T(8,128)(2,1)} %bitcast.16), calls=%async_computation.1 | async-start | bytes 4194304 | tf_op jit(solution)/shard_map/all_to_all | solution.py:18
Sparse Core Ops, SparseCore 0:
  10.4 22.5 all-gather.3
  42.4 29.2 reduce-scatter.2
Sparse Core Ops, SparseCore 1:
  46.2 63.3 all-gather.5
  169.9 81.1 all-gather.7
  253.9 48.9 reduce-scatter.4
where the time goes:
time: 311 us; the launch traced here: 310 us
  waiting for transfers between devices  184 us (59%)
  blocking collectives  61.4 us (20%)
  matrix products  28.1 us (9%)
  between operations  16.4 us (5%)
  local copies, waits for them, and re-layouts  12.8 us (4%)
  starting transfers between devices  4.7 us (2%)
    all_to_all x1, waiting for transfers between devices, on_device(): slices = lax.all_to_all(features, group, 1, 0, tiled=True)  74.7 us
    psum x1, blocking collectives, on_device(): lax.psum((jnp.sum(expo, axis=0), jnp.sum(picked, axis=0)), every)  39.3 us
    all_gather x1, waiting for transfers between devices, on_device(): chat = lax.all_gather(chat_local, every, axis=0, tiled=True)  36.8 us
    reduce_scatter x1, waiting for transfers between devices, on_device(): emb = lax.psum_scatter(part, 'col', scatter_dimension=0, tiled=True)  28.3 us
    all_gather x1, waiting for transfers between devices, on_device(): lax.all_gather(w_in, 'row', axis=0, tiled=True)  24.2 us
    reduce_scatter x1, waiting for transfers between devices, on_device(): lax.psum_scatter(head_term, group, scatter_dimension=1, tiled=True)  19.6 us
    all_gather x1, blocking collectives, on_device(): demb = lax.all_gather(demb, 'col', axis=0, tiled=True)  11.6 us
    unnamed x1, blocking collectives  10.5 us
  transfers between devices with their start and end apart: 6, of which 5 were waited for; matrix products, arithmetic and copies ran while one was open for 8% of the time, Pallas kernels for 0%

commit v1 on v0

--- a/solution.py
+++ b/solution.py
@@ -5,6 +5,21 @@
 
 SCALE = 50.0
 EPS = 1e-06
+
+
+def _start_figure(z):
+    axis_len = lax.axis_size("col")
+    now = z
+    so_far_all = [now]
+    far_arr = [(i0 - 1, i0) for i0 in range(1, axis_len)] + [(axis_len - 1, 0)]
+    for _ in tuple(range(axis_len - 1)):
+        now = lax.ppermute(now, perm=far_arr, axis_name="col")
+        so_far_all += [now]
+    return jnp.roll(
+        jnp.concatenate([*reversed(so_far_all)], axis=0),
+        (lax.axis_index("col") + 1) * now.shape[0],
+        axis=0,
+    )
 
 
 def gelu_back(pre, grad):
@@ -53,7 +68,7 @@
     demb = ((dfhat - fhat * jnp.sum(fhat * dfhat, axis=1, keepdims=True)) * inv).astype(
         jnp.bfloat16
     )
-    demb = lax.all_gather(demb, "col", axis=0, tiled=True)
+    demb = _start_figure(demb)
     dh = lax.dot_general(demb, w_out, (((1,), (1,)), ((), ())), preferred_element_type=f32)
     dpre = gelu_back(pre, dh).astype(jnp.bfloat16)
     dpre_all = lax.all_gather(dpre, group, axis=0, tiled=True)

time: 311 us -> 322 us (1.035)
  waiting for transfers between devices: 184 us -> 201 us
  blocking collectives: 61.4 us -> 49.7 us
    ppermute x0 -> x3, waiting for transfers between devices: none -> 15.4 us  [_start_figure(): now = lax.ppermute(now, perm=far_arr, axis_name='col')]
    all_gather x1 -> x0, blocking collectives: 11.6 us -> none  [on_device(): demb = lax.all_gather(demb, 'col', axis=0, tiled=True)]
    unnamed x18 -> x25, local copies, waits for them, and re-layouts: 8.7 us -> 10.5 us
  transfers between devices with their start and end apart: 6 -> 9, of which waited for: 5 -> 8; matrix products, arithmetic and copies ran while one was open for 8% -> 8% of each run, Pallas kernels for 0% -> 0%
where the time goes in v1:
time: 322 us
  waiting for transfers between devices  201 us (62%)
  blocking collectives  49.7 us (15%)
  matrix products  28.8 us (9%)
  between operations  16.5 us (5%)
  local copies, waits for them, and re-layouts  14.5 us (5%)
  starting transfers between devices  7.76 us (2%)
  other arithmetic  3.44 us (1%)
    all_to_all x1, waiting for transfers between devices, on_device(): slices = lax.all_to_all(features, group, 1, 0, tiled=True)  75.2 us
    psum x1, blocking collectives, on_device(): lax.psum((jnp.sum(expo, axis=0), jnp.sum(picked, axis=0)), every)  39.3 us
    all_gather x1, waiting for transfers between devices, on_device(): chat = lax.all_gather(chat_local, every, axis=0, tiled=True)  36.8 us
    reduce_scatter x1, waiting for transfers between devices, on_device(): emb = lax.psum_scatter(part, 'col', scatter_dimension=0, tiled=True)  28.3 us
    all_gather x1, waiting for transfers between devices, on_device(): lax.all_gather(w_in, 'row', axis=0, tiled=True)  24.2 us
    reduce_scatter x1, waiting for transfers between devices, on_device(): lax.psum_scatter(head_term, group, scatter_dimension=1, tiled=True)  20.2 us
    ppermute x3, waiting for transfers between devices, _start_figure(): now = lax.ppermute(now, perm=far_arr, axis_name='col')  15.4 us
    unnamed x25, local copies, waits for them, and re-layouts  10.5 us
  transfers between devices with their start and end apart: 9, of which 8 were waited for; matrix products, arithmetic and copies ran while one was open for 8% of the time, Pallas kernels for 0%

profile of v1, /device:TPU:0, one launch (start us, length us, event | category | flops | bytes accessed | tf_op | source)
XLA Modules:
  0.0 321.6 jit_solution(14481256050838217552)
XLA Ops:
  8.0 0.0 copy-start
  8.0 0.0 all-gather.4.cloned.1.call-start
  8.1 0.7 all-gather.4.cloned.1.call-update
  8.7 0.0 reduce-scatter.3.cloned.1.call-start
  8.8 24.2 %all-gather.4.cloned.1.call-done = bf16[4096,1024]{1,0:T(8,128)(2,1)} async-done(((bf16[2048,1024]{1,0:T(8,128)(2,1)}), bf16[4096,1024]{1,0:T(8,128)(2,1)}) %all-gather.4.cloned.1.call-update) | async-done | bytes 8388624 | tf_op jit(solution)/shard_map/all_gather | solution.py:40
  33.0 6.3 %fusion.29 = f32[256,1024]{1,0:T(8,128)S(1)} fusion(bf16[256,4096]{1,0:T(8,128)(2,1)} %param.5, bf16[4096,1024]{1,0:T(8,128)(2,1)} %all-gather.4.cloned.1.call-done), kind=kOutput, calls=%fused_computation.56 | convolution fusion | flops 2147483648 | bytes 11534336 | tf_op jit(solution)/shard_map/dot_general | solution.py:39
  39.3 0.0 copy-done
  39.3 0.0 copy-start.2
  39.3 0.0 copy-start.5
  39.4 1.8 fusion.28
  41.2 0.0 reduce-scatter.3.cloned.1.call-update
  41.2 0.0 all-gather.6.cloned.1.call-start
  41.2 0.0 copy-done.2
  41.2 0.1 fusion.16
  41.4 0.8 fusion.17
  42.1 0.0 all-gather.6.cloned.1.call-update
  42.2 0.0 all-gather.8.cloned.1.call-start
  42.2 0.0 copy-done.5
  42.2 0.1 dynamic_slice.10
  42.3 28.3 %reduce-scatter.3.cloned.1.call-done = f32[64,1024]{1,0:T(8,128)} async-done(((f32[256,1024]{1,0:T(8,128)}), f32[64,1024]{1,0:T(8,128)}) %reduce-scatter.3.cloned.1.call-update) | async-done | bytes 262160 | tf_op jit(solution)/shard_map/reduce_scatter | solution.py:44
  70.6 1.1 multiply_reduce_fusion.1
  71.7 0.0 copy-start.1
  71.7 36.8 %all-gather.6.cloned.1.call-done = bf16[2048,1024]{1,0:T(8,128)(2,1)} async-done(((bf16[64,1024]{1,0:T(8,128)(2,1)}), bf16[2048,1024]{1,0:T(8,128)(2,1)}) %all-gather.6.cloned.1.call-update) | async-done | bytes 4194320 | tf_op jit(solution)/shard_map/all_gather | solution.py:38
  108.5 4.6 %fusion.8 = (f32[2048]{0:T(1024)S(1)}, f32[64]{0:T(128)S(1)}, f32[2048]{0:T(1024)S(1)}, f32[64]{0:T(128)S(1)}, f32[64,2048]{1,0:T(8,128)}) fusion(s32[64]{0:T(128)S(1)} %dynamic_slice.10, bf16[2048,1024]{1,0:T(8,128)(2,1)} %all-gather.6.cloned.1.call-done, f32[64,1024]{1,0:T(8,128)} %reduce-scatter.3.cloned.1.call-done, f32[64]{0:T(128)S(1)} %add_rsqrt_fusion.1), kind=kOutput, calls=%fused_computation.16 | convolution fusion | flops 269479808 | bytes 4998144 | tf_op jit(solution)/shard_map/dot_general | solution.py:49
  113.1 39.3 %all-reduce.1 = (f32[2048]{0:T(1024)}, f32[2048]{0:T(1024)S(1)}) all-reduce(f32[2048]{0:T(1024)S(1)} %get-tuple-element.16, f32[2048]{0:T(1024)S(1)} %get-tuple-element.18), channel_id=1, replica_groups=mesh['dp'=4,'row'=2,'col'=4] {'dp','row','col'}, use_global_device_ids=true, to_apply=%region_8.0 | all-reduce | flops 4096 | bytes 32768 | tf_op jit(solution)/shard_map/psum | solution.py:59
  152.4 0.0 copy-start.4
  152.4 0.0 copy-done.1
  152.4 3.4 %multiply_reduce_fusion = (f32[64]{0:T(128)S(1)}, f32[64,1024]{1,0:T(8,128)S(1)}) fusion(f32[64,1024]{1,0:T(8,128)S(1)} %copy-done.1, f32[64]{0:T(128)S(1)} %add_rsqrt_fusion.1, bf16[2048,1024]{1,0:T(8,128)(2,1)} %all-gather.6.cloned.1.call-done, f32[64,2048]{1,0:T(8,128)} %get-tuple-element.22, f32[2048]{0:T(1024)S(1)} %get-tuple-element.21, ...), kind=kOutput, calls=%fused_computation.29 | convolution fusion | flops 269615040 | bytes 5252096 | tf_op jit(solution)/shard_map/dot_general | solution.py:67
  155.8 0.0 copy-done.4
  155.8 0.1 multiply_convert_fusion.1
  155.9 2.3 collective-permute-start
  158.2 4.2 %collective-permute-done = bf16[64,1024]{1,0:T(8,128)(2,1)S(1)} collective-permute-done((bf16[64,1024]{1,0:T(8,128)(2,1)S(1)}, bf16[64,1024]{1,0:T(8,128)(2,1)S(1)}, u32[]{:S(2)}, u32[]{:S(2)}) %collective-permute-start) | collective-permute-done | bytes 131104 | tf_op jit(solution)/shard_map/ppermute | solution.py:16
  162.5 0.7 collective-permute-start.1
  163.2 5.2 %collective-permute-done.1 = bf16[64,1024]{1,0:T(8,128)(2,1)S(1)} collective-permute-done((bf16[64,1024]{1,0:T(8,128)(2,1)S(1)}, bf16[64,1024]{1,0:T(8,128)(2,1)S(1)}, u32[]{:S(2)}, u32[]{:S(2)}) %collective-permute-start.1) | collective-permute-done | bytes 131104 | tf_op jit(solution)/shard_map/ppermute | solution.py:16
  168.4 0.0 collective-permute-start.2
  168.4 6.0 %collective-permute-done.2 = bf16[64,1024]{1,0:T(8,128)(2,1)} collective-permute-done((bf16[64,1024]{1,0:T(8,128)(2,1)S(1)}, bf16[64,1024]{1,0:T(8,128)(2,1)}, u32[]{:S(2)}, u32[]{:S(2)}) %collective-permute-start.2) | collective-permute-done | bytes 131104 | tf_op jit(solution)/shard_map/ppermute | solution.py:16
  174.4 0.9 constant_dynamic-update-slice_fusion.7
  175.4 0.9 constant_dynamic-update-slice_fusion.3
  176.3 0.0 copy-start.3
  176.4 1.0 copy-done.3
  177.3 2.1 fusion.6
  179.4 0.0 all-gather.8.cloned.1.call-update
  179.4 0.0 reduce-scatter.5.cloned.1.call-start
  179.5 3.9 %fusion.10 = f32[1024,1024]{1,0:T(8,128)} fusion(bf16[512,1024]{1,0:T(8,128)(2,1)} %copy-done.3, s32[]{:T(128)S(6)} %select_n.22, f32[256,1024]{1,0:T(8,128)S(1)} %fusion.29), kind=kOutput, calls=%fused_computation.20 | convolution fusion | flops 539230208 | bytes 5767172 | tf_op jit(solution)/shard_map/dot_general | solution.py:75
  183.4 0.0 reduce-scatter.5.cloned.1.call-update
  183.4 4.1 %copy.11 = bf16[256,4096]{0,1:T(8,128)(2,1)} copy(bf16[256,4096]{1,0:T(8,128)(2,1)} %param.5) | data formatting | bytes 4194304 | tf_op args[0]
  187.5 0.0 copy-start.6
  187.5 4.5 %all-to-all-start = ((bf16[256,8,512]{0,2,1:T(8,128)(2,1)}), bf16[256,8,512]{0,2,1:T(8,128)(2,1)}, u32[]{:S(2)}, u32[]{:S(2)}) async-start(bf16[256,8,512]{0,2,1:T(8,128)(2,1)} %bitcast.14), calls=%async_computation.1 | async-start | bytes 4194304 | tf_op jit(solution)/shard_map/all_to_all | solution.py:33
  192.0 0.0 copy-done.6
  192.0 0.6 dynamic-slice
  193.3 75.2 %all-to-all-done = bf16[256,8,512]{0,2,1:T(8,128)(2,1)} async-done(((bf16[256,8,512]{0,2,1:T(8,128)(2,1)}), bf16[256,8,512]{0,2,1:T(8,128)(2,1)}, u32[]{:S(2)}, u32[]{:S(2)}) %all-to-all-start) | async-done | bytes 2097184 | tf_op jit(solution)/shard_map/all_to_all | solution.py:33
  268.5 3.9 %copy.12 = bf16[8,256,512]{2,1,0:T(8,128)(2,1)} copy(bf16[8,256,512]{1,2,0:T(8,128)(2,1)} %bitcast.2) | data formatting | bytes 4194304 | tf_op jit(solution)/shard_map/all_to_all | solution.py:33
  272.4 0.1 subtract_dynamic-update-slice_fusion
  272.5 10.4 %all-reduce = f32[256]{0:T(256)} all-reduce(f32[256]{0:T(256)S(1)} %subtract_dynamic-update-slice_fusion), channel_id=1, replica_groups=mesh['dp'=4,'row'=2,'col'=4] {'col'}, use_global_device_ids=true, to_apply=%add | all-reduce | flops 256 | bytes 2048
  282.9 1.3 dynamic-slice_subtract_fusion
  284.2 0.0 all-gather.8.cloned.1.call-done
  284.2 6.7 %convolution_bitcast_fusion = f32[512,1024]{0,1:T(8,128)} fusion(bf16[2048,1024]{1,0:T(8,128)(2,1)} %all-gather.8.cloned.1.call-done, bf16[2048,512]{1,0:T(8,128)(2,1)} %bitcast.15), kind=kOutput, calls=%fused_computation.1 | convolution fusion | flops 2147483648 | bytes 8388608 | tf_op jit(solution)/shard_map/dot_general | solution.py:77
  290.9 2.9 copy.13
  293.8 20.2 %reduce-scatter.5.cloned.1.call-done = f32[1024,128]{1,0:T(8,128)} async-done(((f32[1024,1024]{1,0:T(8,128)}), f32[1024,128]{1,0:T(8,128)}) %reduce-scatter.5.cloned.1.call-update) | async-done | bytes 524304 | tf_op jit(solution)/shard_map/reduce_scatter | solution.py:76
  (9 shorter events, 0.1 us)
Async XLA Ops:
  8.0 31.3 %copy-start = (bf16[1024,1024]{1,0:T(8,128)(2,1)S(1)}, bf16[1024,1024]{1,0:T(8,128)(2,1)}, u32[]{:S(2)}) copy-start(bf16[1024,1024]{1,0:T(8,128)(2,1)} %param.7) | copy-start | bytes 6291460
  8.0 25.0 %all-gather.4.cloned.1.call-start = ((), (), s32[]{:S(2)}) async-start(), calls=%async_computation.3 | async-start | bytes 12582912 | tf_op jit(solution)/shard_map/all_gather | solution.py:40
  8.7 61.8 %reduce-scatter.3.cloned.1.call-start = ((), (), s32[]{:S(2)}) async-start(), calls=%async_computation.4 | async-start | bytes 1310720 | tf_op jit(solution)/shard_map/reduce_scatter | solution.py:44
  39.3 1.9 copy-start.2
  39.3 2.9 copy-start.5
  41.2 67.3 %all-gather.6.cloned.1.call-start = ((), (), s32[]{:S(2)}) async-start(), calls=%async_computation.5 | async-start | bytes 4325376 | tf_op jit(solution)/shard_map/all_gather | solution.py:38
  42.2 242.0 %all-gather.8.cloned.1.call-start = ((), (), s32[]{:S(2)}) async-start(), calls=%async_computation.6 | async-start | bytes 4718592 | tf_op jit(solution)/shard_map/all_gather | solution.py:74
  71.7 80.7 %copy-start.1 = (f32[64,1024]{1,0:T(8,128)S(1)}, f32[64,1024]{1,0:T(8,128)}, u32[]{:S(2)}) copy-start(f32[64,1024]{1,0:T(8,128)} %reduce-scatter.3.cloned.1.call-done) | copy-start | bytes 786436
  152.4 3.4 %copy-start.4 = (f32[2048]{0:T(1024)}, f32[2048]{0:T(1024)S(1)}, u32[]{:S(2)}) copy-start(f32[2048]{0:T(1024)S(1)} %get-tuple-element.21) | copy-start | bytes 24580
  155.9 6.6 %collective-permute-start = (bf16[64,1024]{1,0:T(8,128)(2,1)S(1)}, bf16[64,1024]{1,0:T(8,128)(2,1)S(1)}, u32[]{:S(2)}, u32[]{:S(2)}) collective-permute-start(bf16[64,1024]{1,0:T(8,128)(2,1)S(1)} %multiply_convert_fusion.1), channel_id=1, source_target_pairs={{0,1},{1,2},{2,3},{3,0},{4,5},{5,6},{6,7},{7,4},{8,9},{9,10},{10,1... | collective-permute-start | bytes 393224 | tf_op jit(solution)/shard_map/ppermute | solution.py:16
  162.5 6.0 %collective-permute-start.1 = (bf16[64,1024]{1,0:T(8,128)(2,1)S(1)}, bf16[64,1024]{1,0:T(8,128)(2,1)S(1)}, u32[]{:S(2)}, u32[]{:S(2)}) collective-permute-start(bf16[64,1024]{1,0:T(8,128)(2,1)S(1)} %collective-permute-done), channel_id=1, source_target_pairs={{0,1},{1,2},{2,3},{3,0},{4,5},{5,6},{6,7},{7,4},{8,9},{9,10},{10,1... | collective-permute-start | bytes 393224 | tf_op jit(solution)/shard_map/ppermute | solution.py:16
  168.4 6.0 %collective-permute-start.2 = (bf16[64,1024]{1,0:T(8,128)(2,1)S(1)}, bf16[64,1024]{1,0:T(8,128)(2,1)}, u32[]{:S(2)}, u32[]{:S(2)}) collective-permute-start(bf16[64,1024]{1,0:T(8,128)(2,1)S(1)} %collective-permute-done.1), channel_id=1, source_target_pairs={{0,1},{1,2},{2,3},{3,0},{4,5},{5,6},{6,7},{7,4},{8,9},{9,10},{10,1... | collective-permute-start | bytes 393224 | tf_op jit(solution)/shard_map/ppermute | solution.py:16
  176.3 1.0 copy-start.3
  179.4 134.5 %reduce-scatter.5.cloned.1.call-start = ((), (), s32[]{:S(2)}) async-start(), calls=%async_computation.7 | async-start | bytes 4718592 | tf_op jit(solution)/shard_map/reduce_scatter | solution.py:76
  187.5 4.5 %copy-start.6 = (u32[32]{0:T(128)S(1)}, u32[32]{0:T(128)}, u32[]{:S(2)}) copy-start(u32[32]{0:T(128)} %constant.71) | copy-start | bytes 388
  187.5 81.0 %all-to-all-start = ((bf16[256,8,512]{0,2,1:T(8,128)(2,1)}), bf16[256,8,512]{0,2,1:T(8,128)(2,1)}, u32[]{:S(2)}, u32[]{:S(2)}) async-start(bf16[256,8,512]{0,2,1:T(8,128)(2,1)} %bitcast.14), calls=%async_computation.1 | async-start | bytes 4194304 | tf_op jit(solution)/shard_map/all_to_all | solution.py:33
Sparse Core Ops, SparseCore 0:
  10.4 22.5 all-gather.3
  41.3 29.2 reduce-scatter.2
Sparse Core Ops, SparseCore 1:
  45.1 63.3 all-gather.5
  179.5 81.7 all-gather.7
  264.1 49.8 reduce-scatter.4
